TPU v7x, 32 devices: a whole 2x2x4 slice. The times are simulated.
32 devices in a mesh: pos: 16 (over z, y, x), head: 2 (over core).
Axes of the slice: x: 2, y: 2, z: 4, core: 2. Of those that a mesh axis runs over, the one named last changes fastest.
Arguments:
- inputs: bfloat16 [16384, 1024], P('pos'), may hold values from -400 to 400
- valid_blocks: int32 [128], P('pos'), may hold values from 0 to 1, as said below
- latents: bfloat16 [2048, 1024], P('pos'), may hold values from -6 to 6
- w_query: bfloat16 [1024, 1024], P(None, 'head'), may hold values from -0.1875 to 0.1875
- w_key: bfloat16 [1024, 1024], P(None, 'head'), may hold values from -0.1875 to 0.1875
- w_value: bfloat16 [1024, 1024], P(None, 'head'), may hold values from -0.1875 to 0.1875
- w_out: bfloat16 [1024, 1024], P('head'), may hold values from -0.1875 to 0.1875
- w_mlp: bfloat16 [1024, 1024], replicated, may hold values from -0.1875 to 0.1875
- w_lkey: bfloat16 [1024, 1024], P(None, 'head'), may hold values from -0.1875 to 0.1875
- w_lvalue: bfloat16 [1024, 1024], P(None, 'head'), may hold values from -0.1875 to 0.1875
- w_pquery: bfloat16 [1024, 1024], P(None, 'head'), may hold values from -0.1875 to 0.1875
- w_pout: bfloat16 [1024, 1024], P('head'), may hold values from -0.1875 to 0.1875
Outputs:
- decoded: bfloat16 [16384, 1024], P(('pos', 'head'))
Inputs may be any that keep to these rules, and one draw needn't show every extreme that they name: `valid_blocks`: within the 1024 positions of each device the blocks marked 1 come first; every device has at least one block marked 1, and some device has all its blocks marked 1.
All inputs are finite; a program needn't handle non-finite values.
Results may differ from a plain program's by a relative error of at most 0.017.
The roundings to bfloat16 on the way count: a program that leaves them out, or rounds other values in their place, can miss the bound.
Values may be sent and summed in bfloat16 or wider, within the bound.
A program may use at most 128 MiB of HBM per device.

v0:
```python
import jax
import jax.numpy as jnp
from jax import lax
from jax.sharding import PartitionSpec as P

HEAD_DIM = 128
LAT = 2048
BLK = 128


masked_score = -1e30
epsilon = 1e-05


def rms_norm(values):
    return values * lax.rsqrt(jnp.mean(values * values, axis=-1, keepdims=True) + epsilon)


def per_device(
    inputs,
    valid_blocks,
    latents,
    w_query,
    w_key,
    w_value,
    w_out,
    w_mlp,
    w_lkey,
    w_lvalue,
    w_pquery,
    w_pout,
):
    scaling = HEAD_DIM ** (-0.5)
    pos_local = inputs.shape[0]
    lat_local = latents.shape[0]
    heads_local = w_key.shape[1] // HEAD_DIM
    columns = heads_local * HEAD_DIM
    pos_keys = (
        jnp.dot(inputs, w_key, preferred_element_type=jnp.float32)
        .astype(jnp.bfloat16)
        .reshape(pos_local, heads_local, HEAD_DIM)
    )
    pos_values = (
        jnp.dot(inputs, w_value, preferred_element_type=jnp.float32)
        .astype(jnp.bfloat16)
        .reshape(pos_local, heads_local, HEAD_DIM)
    )
    own_queries = jnp.dot(latents, w_query, preferred_element_type=jnp.float32).astype(jnp.bfloat16)
    lat_queries = lax.all_gather(own_queries, "pos", axis=0, tiled=True).reshape(
        LAT, heads_local, HEAD_DIM
    )
    alive_mask = jnp.repeat(valid_blocks, BLK) > 0
    lat_block = min(LAT, 1024)

    def cross_block(query_rows):
        scores = (
            jnp.einsum("lhe,phe->lhp", query_rows, pos_keys, preferred_element_type=jnp.float32)
            * scaling
        )
        scores = jnp.where(alive_mask[None, None, :], scores, masked_score)
        row_max = jnp.max(scores, axis=-1)
        exponent = jnp.exp(scores - row_max[..., None])
        totals = jnp.sum(exponent, axis=-1)
        sums = jnp.einsum(
            "lhp,phe->lhe",
            exponent.astype(jnp.bfloat16),
            pos_values,
            preferred_element_type=jnp.float32,
        )
        return (row_max, totals, sums)

    row_max, totals, sums = lax.map(
        cross_block, lat_queries.reshape(LAT // lat_block, lat_block, heads_local, HEAD_DIM)
    )
    row_max = row_max.reshape(LAT, heads_local)
    totals = totals.reshape(LAT, heads_local)
    sums = sums.reshape(LAT, heads_local, HEAD_DIM)
    global_max = lax.pmax(row_max.astype(jnp.bfloat16), "pos").astype(row_max.dtype)
    factor = jnp.exp(row_max - global_max)
    scaled_totals = totals * factor
    scaled_sums = sums * factor[..., None]
    all_totals, all_sums = lax.psum((scaled_totals, scaled_sums), "pos")
    offset = lax.axis_index("pos") * lat_local
    own_totals = lax.dynamic_slice_in_dim(all_totals, offset, lat_local, 0)
    own_sums = lax.dynamic_slice_in_dim(all_sums, offset, lat_local, 0)
    attended = (own_sums / own_totals[..., None]).astype(jnp.bfloat16).reshape(lat_local, columns)
    partial_terms = jnp.dot(attended, w_out, preferred_element_type=jnp.float32)
    merged = lax.psum(partial_terms.astype(jnp.bfloat16), "head").astype(jnp.float32)
    normed = rms_norm(merged)
    hidden = jax.nn.gelu(
        jnp.dot(normed.astype(jnp.bfloat16), w_mlp, preferred_element_type=jnp.float32)
    )
    lat_rows = (normed + hidden).astype(jnp.bfloat16)
    lat_keys = jnp.dot(lat_rows, w_lkey, preferred_element_type=jnp.float32).astype(jnp.bfloat16)
    lat_values = jnp.dot(lat_rows, w_lvalue, preferred_element_type=jnp.float32).astype(
        jnp.bfloat16
    )
    query_block = min(pos_local, 512)
    pos_queries = jnp.dot(inputs, w_pquery, preferred_element_type=jnp.float32).astype(jnp.bfloat16)
    pos_queries = pos_queries.reshape(pos_local // query_block, query_block, heads_local, HEAD_DIM)
    shape_rows = (pos_local // query_block, query_block, heads_local)
    initial = (
        jnp.full(shape_rows, masked_score, jnp.float32),
        jnp.zeros(shape_rows, jnp.float32),
        jnp.zeros(shape_rows + (HEAD_DIM,), jnp.float32),
    )
    piece_keys = lax.all_gather(lat_keys, "pos", axis=0, tiled=True).reshape(
        -1, heads_local, HEAD_DIM
    )
    piece_values = lax.all_gather(lat_values, "pos", axis=0, tiled=True).reshape(
        -1, heads_local, HEAD_DIM
    )

    def one_block(operands):
        query_rows, old_max, old_totals, old_sums = operands
        scores = (
            jnp.einsum("phe,lhe->phl", query_rows, piece_keys, preferred_element_type=jnp.float32)
            * scaling
        )
        new_max = jnp.maximum(old_max, jnp.max(scores, axis=-1))
        keeping = jnp.exp(old_max - new_max)
        exponent = jnp.exp(scores - new_max[..., None])
        new_totals = old_totals * keeping + jnp.sum(exponent, axis=-1)
        new_sums = old_sums * keeping[..., None] + jnp.einsum(
            "phl,lhe->phe",
            exponent.astype(jnp.bfloat16),
            piece_values,
            preferred_element_type=jnp.float32,
        )
        return (new_max, new_totals, new_sums)

    final_max, final_totals, final_sums = lax.map(
        one_block, (pos_queries, initial[0], initial[1], initial[2])
    )
    pos_attended = (
        (final_sums / final_totals[..., None]).astype(jnp.bfloat16).reshape(pos_local, columns)
    )
    terms = jnp.dot(pos_attended, w_pout, preferred_element_type=jnp.float32)
    own_rows = lax.psum_scatter(
        terms.astype(jnp.bfloat16), "head", scatter_dimension=0, tiled=True
    ).astype(jnp.float32)
    return rms_norm(own_rows).astype(jnp.bfloat16)


def solution(mesh):
    placed = (
        P("pos", None),
        P("pos"),
        P("pos", None),
        P(None, "head"),
        P(None, "head"),
        P(None, "head"),
        P("head", None),
        P(),
        P(None, "head"),
        P(None, "head"),
        P(None, "head"),
        P("head", None),
    )
    return jax.shard_map(
        per_device, mesh=mesh, in_specs=placed, out_specs=P(("pos", "head"), None), check_vma=False
    )
```

profile of v0, /device:TPU:9, one launch (start us, length us, event | category | flops | bytes accessed | tf_op | source)
XLA Modules:
  0.0 572.3 jit_solution(1721711075635332809)
XLA Ops:
  6.5 2.4 convolution_convert_fusion.7
  8.9 0.0 all-gather.4.cloned.1.call-update
  9.0 0.0 all-reduce.3.cloned.1.call-start
  9.1 3.5 convolution_convert_fusion.2
  12.6 1.6 copy.31
  14.2 0.0 copy-start.8
  14.2 3.5 convolution_convert_fusion.1
  17.7 2.3 copy.32
  20.0 51.5 %all-gather.4.cloned.1.call-done = bf16[2048,512]{1,0:T(8,128)(2,1)} async-done(((bf16[128,512]{1,0:T(8,128)(2,1)}), bf16[2048,512]{1,0:T(8,128)(2,1)}) %all-gather.4.cloned.1.call-update) | async-done | bytes 2097168 | tf_op jit(solution)/shard_map/all_gather | solution.py:49
  71.5 4.0 reshape_reshape.3
  75.4 57.5 %while.28 = (s32[]{:T(128)}, f32[2,1024,4]{1,2,0:T(4,128)S(1)}, f32[2,1024,4]{1,2,0:T(4,128)S(1)}, f32[2,1024,4,128]{3,1,0,2:T(8,128)}, bf16[2,1024,4,128]{3,2,1...) while((s32[]{:T(128)}, f32[2,1024,4]{1,2,0:T(4,128)S(1)}, ...), condition=%wide.region_3.4_spmd.clone, body=%wide.region_0.3_spmd.clone.sunk | while | flops 2193612800 | bytes 57807468 | solution.py:72
  75.4 1.6 constant_dynamic-slice_fusion.6
  77.0 0.1 broadcast_bitcast_fusion.2
  77.1 7.2 %bitcast_reduce_fusion.5 = (f32[1024,4]{0,1:T(4,128)S(1)}, f32[4,1024,1024]{1,2,0:T(8,128)}) fusion(pred[1024]{0:T(1024)(128)(4,1)S(1)} %broadcast_bitcast_fusion.2, bf16[1024,4,128]{2,0,1:T(8,128)(2,1)S(1)} %get-tuple-element.311, bf16[1,1024,4,128]{3,2,1,0:T(4,128)(2,1)S(1)} %constant_dynamic-slice_fusion.6), kind=kOutput, calls=%fused_computation.21.clone.1 | convolution fusion | flops 1086320640 | bytes 18891776 | tf_op jit(solution)/shard_map/while/body/eval_jaxpr/lhe,phe->lhp/dot_general | solution.py:57
  84.3 12.0 %bitcast_dynamic-update-slice_fusion.9 = f32[2,1024,4,128]{3,1,0,2:T(8,128)} fusion(f32[2,1024,4,128]{3,1,0,2:T(8,128)} %get-tuple-element.300, s32[]{:T(128)} %get-tuple-element.297, bf16[1024,4,128]{2,0,1:T(8,128)(2,1)} %get-tuple-element.312, f32[4,1024,1024]{1,2,0:T(8,128)} %get-tuple-element.284, f32[1024,4]{0,1:T(4,128)S(1)} %get-tuple-element.285, ...), kind=kOutput, calls=%fused_computation.28.clone.1 | convolution fusion | flops 1090519040 | bytes 19940864 | tf_op jit(solution)/shard_map/while/body/eval_jaxpr/lhp,phe->lhe/dot_general | solution.py:64
  96.3 7.9 %fusion.94 = f32[1024,4]{0,1:T(4,128)S(1)} fusion(f32[4,1024,1024]{1,2,0:T(8,128)} %get-tuple-element.284, f32[1024,4]{0,1:T(4,128)S(1)} %get-tuple-element.285, pred[1024]{0:T(1024)(128)(4,1)S(1)} %broadcast_bitcast_fusion.2), kind=kLoop, calls=%fused_computation.25.clone.1 | loop fusion | flops 16773120 | bytes 16811008 | tf_op jit(solution)/shard_map/while/body/eval_jaxpr/reduce_sum | solution.py:63
  104.2 1.6 constant_dynamic-slice_fusion.6
  105.8 0.1 broadcast_bitcast_fusion.2
  105.9 7.2 %bitcast_reduce_fusion.5 = (f32[1024,4]{0,1:T(4,128)S(1)}, f32[4,1024,1024]{1,2,0:T(8,128)}) fusion(pred[1024]{0:T(1024)(128)(4,1)S(1)} %broadcast_bitcast_fusion.2, bf16[1024,4,128]{2,0,1:T(8,128)(2,1)S(1)} %get-tuple-element.311, bf16[1,1024,4,128]{3,2,1,0:T(4,128)(2,1)S(1)} %constant_dynamic-slice_fusion.6), kind=kOutput, calls=%fused_computation.21.clone.1 | convolution fusion | flops 1086320640 | bytes 18891776 | tf_op jit(solution)/shard_map/while/body/eval_jaxpr/lhe,phe->lhp/dot_general | solution.py:57
  113.0 12.0 %bitcast_dynamic-update-slice_fusion.9 = f32[2,1024,4,128]{3,1,0,2:T(8,128)} fusion(f32[2,1024,4,128]{3,1,0,2:T(8,128)} %get-tuple-element.300, s32[]{:T(128)} %get-tuple-element.297, bf16[1024,4,128]{2,0,1:T(8,128)(2,1)} %get-tuple-element.312, f32[4,1024,1024]{1,2,0:T(8,128)} %get-tuple-element.284, f32[1024,4]{0,1:T(4,128)S(1)} %get-tuple-element.285, ...), kind=kOutput, calls=%fused_computation.28.clone.1 | convolution fusion | flops 1090519040 | bytes 19940864 | tf_op jit(solution)/shard_map/while/body/eval_jaxpr/lhp,phe->lhe/dot_general | solution.py:64
  125.0 7.9 %fusion.94 = f32[1024,4]{0,1:T(4,128)S(1)} fusion(f32[4,1024,1024]{1,2,0:T(8,128)} %get-tuple-element.284, f32[1024,4]{0,1:T(4,128)S(1)} %get-tuple-element.285, pred[1024]{0:T(1024)(128)(4,1)S(1)} %broadcast_bitcast_fusion.2), kind=kLoop, calls=%fused_computation.25.clone.1 | loop fusion | flops 16773120 | bytes 16811008 | tf_op jit(solution)/shard_map/while/body/eval_jaxpr/reduce_sum | solution.py:63
  132.9 54.2 %pmax.7 = bf16[2048,4]{0,1:T(4,128)(2,1)S(1)} all-reduce(bf16[2048,4]{0,1:T(4,128)(2,1)S(1)} %convert_element_type.61), channel_id=1, replica_groups=mesh['pos'=16,'head'=2] {'pos'}, use_global_device_ids=true, to_apply=%region_4.5 | all-reduce | flops 8192 | bytes 32768 | tf_op jit(solution)/shard_map/pmax | solution.py:78
  187.1 4.1 bitcast_multiply_fusion
  191.3 0.0 all-reduce.3.cloned.1.call-update
  191.3 0.0 all-reduce.5.cloned.1.call-start
  191.3 60.9 %psum.22 = f32[2048,4]{0,1:T(4,128)S(1)} all-reduce(f32[2048,4]{0,1:T(4,128)S(1)} %get-tuple-element.176), channel_id=1, replica_groups=mesh['pos'=16,'head'=2] {'pos'}, use_global_device_ids=true, to_apply=%region_6.7 | all-reduce | flops 8192 | bytes 65536 | tf_op jit(solution)/shard_map/psum | solution.py:82
  252.2 123.6 %all-reduce.3.cloned.1.call-done = f32[2048,4,128]{2,0,1:T(8,128)} async-done(((f32[2048,4,128]{2,0,1:T(8,128)}), f32[2048,4,128]{2,0,1:T(8,128)}) %all-reduce.3.cloned.1.call-update) | async-done | bytes 4194320 | tf_op jit(solution)/shard_map/psum | solution.py:82
  375.8 1.1 divide_convert_fusion.1
  376.9 0.1 copy.34
  377.0 1.0 convolution_convert_fusion.4
  378.1 0.0 all-reduce.5.cloned.1.call-update
  378.1 0.0 all-gather.8.cloned.1.call-start
  378.1 19.7 %all-reduce.5.cloned.1.call-done = bf16[128,1024]{1,0:T(8,128)(2,1)} async-done(((bf16[128,1024]{1,0:T(8,128)(2,1)}), bf16[128,1024]{1,0:T(8,128)(2,1)}) %all-reduce.5.cloned.1.call-update) | async-done | bytes 262160 | tf_op jit(solution)/shard_map/psum | solution.py:88
  397.8 1.1 fusion.41
  398.9 2.2 fusion.40
  401.2 0.9 convolution_convert_fusion.5
  402.1 0.0 all-gather.8.cloned.1.call-update
  402.1 0.0 all-gather.6.cloned.1.call-start
  402.2 2.2 convolution_convert_fusion.6
  404.4 0.0 all-gather.6.cloned.1.call-update
  404.4 0.0 reduce-scatter.2.cloned.1.call-start
  404.5 3.4 convolution_convert_fusion.3
  407.9 1.3 reshape.91
  409.3 53.6 %all-gather.8.cloned.1.call-done = bf16[2048,512]{1,0:T(8,128)(2,1)} async-done(((bf16[128,512]{1,0:T(8,128)(2,1)}), bf16[2048,512]{1,0:T(8,128)(2,1)}) %all-gather.8.cloned.1.call-update) | async-done | bytes 2097168 | tf_op jit(solution)/shard_map/all_gather | solution.py:110
  462.9 3.3 copy_bitcast_fusion.4
  466.2 58.7 %all-gather.6.cloned.1.call-done = bf16[2048,512]{1,0:T(8,128)(2,1)} async-done(((bf16[128,512]{1,0:T(8,128)(2,1)}), bf16[2048,512]{1,0:T(8,128)(2,1)}) %all-gather.6.cloned.1.call-update) | async-done | bytes 2097168 | tf_op jit(solution)/shard_map/all_gather | solution.py:107
  524.9 2.0 copy_bitcast_fusion.5
  526.8 19.4 %while.27 = (s32[]{:T(128)}, f32[2,512,4]{1,2,0:T(4,128)S(1)}, f32[2,512,4,128]{3,1,2,0:T(8,128)}, bf16[2,512,4,128]{3,2,1,0:T(4,128)(2,1)S(1)}, bf16[2048,4,128...) while((s32[]{:T(128)}, f32[2,512,4]{1,2,0:T(4,128)S(1)}, ...), condition=%wide.region_12.13_spmd, body=%wide.region_9.12_spmd.sunk | while | flops 2181310464 | bytes 82403496 | solution.py:132
  526.8 0.2 constant_dynamic-slice_fusion.5
  527.1 2.4 bitcast_reduce_fusion.4
  529.5 3.7 fusion.90
  533.2 3.3 fusion.89
  536.6 0.2 constant_dynamic-slice_fusion.5
  536.8 2.4 bitcast_reduce_fusion.4
  539.2 3.7 fusion.90
  542.9 3.3 fusion.89
  546.2 0.0 copy-start.7
  546.3 2.0 divide_convert_fusion
  548.3 0.8 copy.38
  549.1 2.6 convolution_convert_fusion
  551.8 0.0 reduce-scatter.2.cloned.1.call-update
  551.8 9.7 %reduce-scatter.2.cloned.1.call-done = bf16[512,1024]{1,0:T(8,128)(2,1)} async-done(((bf16[1024,1024]{1,0:T(8,128)(2,1)}), bf16[512,1024]{1,0:T(8,128)(2,1)}) %reduce-scatter.2.cloned.1.call-update) | async-done | bytes 1048592 | tf_op jit(solution)/shard_map/reduce_scatter | solution.py:139
  561.5 1.5 fusion.34
  563.0 2.4 fusion.35
  (40 shorter events, 0.2 us)
Async XLA Ops:
  6.5 2.5 copy-start
  6.5 64.9 %all-gather.4.cloned.1.call-start = ((), (), s32[]{:S(2)}) async-start(), calls=%async_computation.1 | async-start | bytes 2228224 | tf_op jit(solution)/shard_map/all_gather | solution.py:49
  9.0 366.8 %all-reduce.3.cloned.1.call-start = ((), (), s32[]{:S(2)}) async-start(), calls=%async_computation.2 | async-start | bytes 8388608 | tf_op jit(solution)/shard_map/psum | solution.py:82
  14.2 5.8 %copy-start.8 = (s32[8]{0:T(128)S(1)}, s32[8]{0:T(128)}, u32[]{:S(2)}) copy-start(s32[8]{0:T(128)} %param.17) | copy-start | bytes 100
  191.3 185.7 %copy-start.5 = (bf16[512,1024]{1,0:T(8,128)(2,1)S(1)}, bf16[512,1024]{1,0:T(8,128)(2,1)}, u32[]{:S(2)}) copy-start(bf16[512,1024]{1,0:T(8,128)(2,1)} %param.22) | copy-start | bytes 3145732
  191.3 206.5 %all-reduce.5.cloned.1.call-start = ((), (), s32[]{:S(2)}) async-start(), calls=%async_computation.3 | async-start | bytes 524288 | tf_op jit(solution)/shard_map/psum | solution.py:88
  378.0 23.1 %copy-start.6 = (bf16[1024,512]{1,0:T(8,128)(2,1)S(1)}, bf16[1024,512]{1,0:T(8,128)(2,1)}, u32[]{:S(2)}) copy-start(bf16[1024,512]{1,0:T(8,128)(2,1)} %param.25) | copy-start | bytes 3145732
  378.1 84.8 %all-gather.8.cloned.1.call-start = ((), (), s32[]{:S(2)}) async-start(), calls=%async_computation.5 | async-start | bytes 2228224 | tf_op jit(solution)/shard_map/all_gather | solution.py:110
  402.1 122.7 %all-gather.6.cloned.1.call-start = ((), (), s32[]{:S(2)}) async-start(), calls=%async_computation.4 | async-start | bytes 2228224 | tf_op jit(solution)/shard_map/all_gather | solution.py:107
  404.4 157.1 %reduce-scatter.2.cloned.1.call-start = ((), (), s32[]{:S(2)}) async-start(), calls=%async_computation.6 | async-start | bytes 3145728 | tf_op jit(solution)/shard_map/reduce_scatter | solution.py:139
  527.0 2.5 copy-start.2
  527.1 2.5 copy-start.4
  533.2 3.3 copy-start.3
  536.7 2.5 copy-start.2
  536.8 2.5 copy-start.4
  542.9 3.3 copy-start.3
  546.2 2.9 copy-start.7
  549.1 16.3 %copy-start.1 = (bf16[1024,1024]{1,0:T(8,128)(2,1)S(1)}, bf16[1024,1024]{1,0:T(8,128)(2,1)}, u32[]{:S(2)}) copy-start(bf16[1024,1024]{1,0:T(8,128)(2,1)} %param.16) | copy-start | bytes 6291460
Sparse Core Ops, SparseCore 0:
  10.1 61.2 all-gather.3
  191.4 184.3 all-reduce.2
  378.2 19.5 all-reduce.4
  402.3 60.5 all-gather.7
  465.5 59.3 all-gather.5
  551.9 9.5 reduce-scatter.1
where the time goes:
time: 574 us; the launch traced here: 572 us
  waiting for transfers between devices  317 us (55%)
  blocking collectives  115 us (20%)
  matrix products  72.4 us (13%)
  other arithmetic  34.7 us (6%)
  local copies, waits for them, and re-layouts  19.2 us (3%)
  between operations  13.7 us (2%)
    psum x1, waiting for transfers between devices, per_device(): all_totals, all_sums = lax.psum((scaled_totals, scaled_sums), 'pos')  124 us
    psum x1, blocking collectives, per_device(): all_totals, all_sums = lax.psum((scaled_totals, scaled_sums), 'pos')  60.9 us
    all_gather x1, waiting for transfers between devices, per_device(): lax.all_gather(lat_keys, 'pos', axis=0, tiled=True)  58.7 us
    pmax x1, blocking collectives, per_device(): lax.pmax(row_max.astype(jnp.bfloat16), 'pos').astype(row_max.dtype)  54.2 us
    all_gather x1, waiting for transfers between devices, per_device(): lax.all_gather(lat_values, 'pos', axis=0, tiled=True)  53.6 us
    all_gather x1, waiting for transfers between devices, per_device(): lax.all_gather(own_queries, 'pos', axis=0, tiled=True)  51.5 us
    dot_general x2, matrix products, cross_block(): jnp.einsum('lhp,phe->lhe', exponent.astype(jnp.bfloat16), pos_values, pre...  24 us
    psum x1, waiting for transfers between devices, per_device(): lax.psum(partial_terms.astype(jnp.bfloat16), 'head').astype(jnp.float32)  19.7 us
  transfers between devices with their start and end apart: 6, of which 6 were waited for; matrix products, arithmetic and copies ran while one was open for 4% of the time, Pallas kernels for 0%

commit v1 on v0

v1 whole, which is shorter than its diff:
```python
import functools
import math

import jax
import jax.numpy as jnp
from jax import lax
from jax.experimental import pallas as pl
from jax.experimental.pallas import tpu as pltpu
from jax.sharding import PartitionSpec as P

HEAD_DIM = 128
masked_score = -1e30
epsilon = 1e-05
F32 = jnp.float32
BF16 = jnp.bfloat16
MESH = pl.DeviceIdType.MESH
N_STREAMS = 2


def rms_norm(values):
    return values * lax.rsqrt(jnp.mean(values * values, axis=-1, keepdims=True) + epsilon)


def mm(a, b):
    return jnp.dot(a, b, preferred_element_type=F32)


def group(g):
    return (0, 1) if g == 0 else (2 ** (g - 1), 2**g)


def kernel(n, inputs, bias, latents, w_query, w_key, w_value, w_out, w_mlp, w_lkey, w_lvalue,
           w_pquery, w_pout, out,
           v_in, v_bias, v_lat, v_wq, v_wk, v_wv, v_wo, v_wm, v_wlk, v_wlv, v_wpq, v_wpo,
           qt, keys, valt, pqt, osum, stats, orecv, srecv, lr, lkeys, lvalt, pa,
           tsend, trecv, msend, mrecv,
           load_sem, gs_sem, gr_sem, hs_sem, hr_sem, ds_sem, dr_sem,
           os_sem, or_sem, ss_sem, sr_sem, x_sem):
    bits = n.bit_length() - 1
    heads, pos, _ = keys.shape
    hs = heads // N_STREAMS
    lat_local = v_lat.shape[0]
    lat = n * lat_local
    width = v_lat.shape[1]
    scale = HEAD_DIM ** (-0.5) * math.log2(math.e)
    me = lax.axis_index("pos")
    core = lax.axis_index("head")
    high = list(range(bits - 1, 1, -1))
    gather_order = [high + [0, 1], high + [1, 0]]
    reduce_order = [high + [1, 0], high + [0, 1]]

    def partner(bit):
        step = 2**bit
        flipped = me + step - 2 * step * ((me // step) % 2)
        return {"pos": flipped, "head": core}

    other = {"pos": me, "head": 1 - core}

    loads = []
    for i, (src, dst) in enumerate([
        (latents, v_lat), (w_query, v_wq), (inputs, v_in), (w_key, v_wk), (w_value, v_wv),
        (bias, v_bias), (w_pquery, v_wpq), (w_out, v_wo), (w_mlp, v_wm), (w_lkey, v_wlk),
        (w_lvalue, v_wlv), (w_pout, v_wpo),
    ]):
        copy = pltpu.make_async_copy(src, dst, load_sem.at[i])
        copy.start()
        loads.append(copy)

    barrier = pltpu.get_barrier_semaphore()
    for bit in range(bits):
        pl.semaphore_signal(barrier, inc=1, device_id=partner(bit), device_id_type=MESH)
    pl.semaphore_signal(barrier, inc=1, device_id=other, device_id_type=MESH)
    pl.semaphore_wait(barrier, bits + 1)

    def remote(src, dst, send, recv, device):
        return pltpu.make_async_remote_copy(
            src_ref=src, dst_ref=dst, send_sem=send, recv_sem=recv, device_id=device,
            device_id_type=MESH)

    class Gather:
        def __init__(self, view, send, recv):
            self.copies = {}
            for s in range(N_STREAMS):
                for t in range(bits):
                    for g in range(t + 1):
                        a, b = group(g)
                        self.copies[s, t, g] = remote(
                            view(s, a, b), view(s, 2**t + a, 2**t + b),
                            send.at[s, t, g], recv.at[s, t, g], partner(gather_order[s][t]))

        def ready(self, g):
            for s in range(N_STREAMS):
                if g > 0:
                    for i in range(g):
                        self.copies[s, g - 1, i].wait_recv()
                for t in range(g, bits):
                    self.copies[s, t, g].start()

        def finish(self):
            for copy in self.copies.values():
                copy.wait_send()

    loads[0].wait()
    loads[1].wait()
    own = mm(v_lat[...], v_wq[...]).T.astype(BF16)
    for h in range(heads):
        qt[h // hs, 0, h % hs] = own[h * HEAD_DIM:(h + 1) * HEAD_DIM]
    gather_q = Gather(lambda s, a, b: qt.at[s, a:b], gs_sem, gr_sem)
    gather_q.ready(0)

    rows = min(pos, 256)

    def project(weight, store):
        def body(i, _):
            start = pl.multiple_of(i * rows, rows)
            store(start, mm(v_in[pl.ds(start, rows)], weight[...]))
            return 0
        lax.fori_loop(0, pos // rows, body, 0)

    def store_keys(start, value):
        for h in range(heads):
            keys[h, pl.ds(start, rows)] = value[:, h * HEAD_DIM:(h + 1) * HEAD_DIM].astype(BF16)

    def store_transposed(dst):
        def store(start, value):
            flipped = value.T.astype(BF16)
            for h in range(heads):
                dst[h, :, pl.ds(start, rows)] = flipped[h * HEAD_DIM:(h + 1) * HEAD_DIM]
        return store

    loads[2].wait()
    loads[3].wait()
    project(v_wk, store_keys)
    gather_q.ready(1)
    loads[4].wait()
    project(v_wv, store_transposed(valt))
    gather_q.ready(2)

    def attend(key, query, value, extra):
        scores = mm(key, query) * scale
        if extra is not None:
            scores = scores + extra
        top = jnp.max(scores, axis=0, keepdims=True)
        exponent = jnp.exp2(scores - top)
        total = jnp.sum(exponent, axis=0, keepdims=True)
        return top, total, mm(value, exponent.astype(BF16))

    pair = 2 if lat_local % 128 == 0 else 1
    quarter = n // 4

    def encode(q):
        target = {0: 0, 1: 2, 2: 1, 3: 3}[q]

        def body(i, _):
            h = i % heads
            r = (i // heads) * pair
            s, hh = h // hs, h % hs
            src, dst = q * quarter + r, target * quarter + r
            query = [qt[s, src + j, hh] for j in range(pair)]
            extra = [v_bias[...]] * pair
            top, total, summed = attend(
                keys[h], jnp.concatenate(query, axis=1) if pair > 1 else query[0],
                valt[h], jnp.concatenate(extra, axis=1) if pair > 1 else extra[0])
            summed = summed.astype(BF16)
            for j in range(pair):
                cut = slice(j * lat_local, (j + 1) * lat_local)
                osum[s, dst + j, hh] = summed[:, cut]
                stats[s, dst + j, hh, 0:1] = top[:, cut]
                stats[s, dst + j, hh, 1:2] = total[:, cut]
            return 0

        lax.fori_loop(0, heads * quarter // pair, body, 0)

    sent = []

    def reduce_copies(t, part, a, b, base):
        copies = []
        for s in range(N_STREAMS):
            device = partner(reduce_order[s][t])
            copies.append((
                remote(osum.at[s, a:b], orecv.at[s, base:base + b - a],
                       os_sem.at[s, t, part], or_sem.at[s, t, part], device),
                remote(stats.at[s, a:b], srecv.at[s, base:base + b - a],
                       ss_sem.at[s, t, part], sr_sem.at[s, t, part], device)))
        for o, st in copies:
            o.start()
            st.start()
        sent.extend(copies)
        return copies

    def merge(copies, a, b, base):
        for o, st in copies:
            o.wait_recv()
            st.wait_recv()

        def body(i, _):
            h = i % heads
            r = i // heads
            s, hh = h // hs, h % hs
            mine, theirs = stats[s, a + r, hh], srecv[s, base + r, hh]
            top = jnp.maximum(mine[0:1], theirs[0:1])
            f, g = jnp.exp2(mine[0:1] - top), jnp.exp2(theirs[0:1] - top)
            stats[s, a + r, hh, 0:1] = top
            stats[s, a + r, hh, 1:2] = mine[1:2] * f + theirs[1:2] * g
            osum[s, a + r, hh] = (
                osum[s, a + r, hh].astype(F32) * f + orecv[s, base + r, hh].astype(F32) * g
            ).astype(BF16)
            return 0

        lax.fori_loop(0, heads * (b - a), body, 0)

    loads[5].wait()
    encode(0)
    gather_q.ready(3)
    for g in range(4, bits):
        gather_q.ready(g)
    if bits == 4:
        encode(1)
        early = reduce_copies(3, 0, 2 * quarter, 3 * quarter, quarter)
        gather_q.ready(bits)
    else:
        gather_q.ready(bits)
        encode(1)
        early = reduce_copies(bits - 1, 0, 2 * quarter, 3 * quarter, quarter)
    encode(3)
    late = reduce_copies(bits - 1, 1, 3 * quarter, n, 0)
    encode(2)
    merge(late, quarter, 2 * quarter, 0)
    base = 2 * quarter
    step = reduce_copies(bits - 2, 0, quarter, 2 * quarter, base)
    loads[6].wait()
    project(v_wpq, store_transposed(pqt))
    merge(early, 0, quarter, quarter)
    merge(step, 0, quarter, base)
    base += quarter
    for t in range(bits - 3, -1, -1):
        step = reduce_copies(t, 0, 2**t, 2 ** (t + 1), base)
        merge(step, 0, 2**t, base)
        base += 2**t
    gather_q.finish()

    attended = []
    for h in range(heads):
        s, hh = h // hs, h % hs
        attended.append((osum[s, 0, hh].astype(F32) / stats[s, 0, hh][1:2]).T.astype(BF16))
    loads[7].wait()
    partial = mm(jnp.concatenate(attended, axis=1), v_wo[...]).astype(BF16)
    msend[...] = partial
    swap = remote(msend, mrecv, x_sem.at[0], x_sem.at[1], other)
    swap.start()
    loads[8].wait()
    swap.wait()
    normed = rms_norm(msend[...].astype(F32) + mrecv[...].astype(F32))
    hidden = jax.nn.gelu(mm(normed.astype(BF16), v_wm[...]))
    lat_rows = (normed + hidden).astype(BF16)
    parts = lr.shape[0]
    span = width // parts
    for q in range(parts):
        lr[q, 0] = lat_rows[:, q * span:(q + 1) * span]

    gather_l = Gather(lambda s, a, b: lr.at[core * N_STREAMS + s, a:b], hs_sem, hr_sem)
    gather_l.ready(0)
    shares = {}
    for g in range(1, bits + 1):
        gather_l.ready(g)
        a, b = group(g)
        for s in range(N_STREAMS):
            view = lr.at[core * N_STREAMS + s, a:b]
            shares[s, g] = remote(view, view, ds_sem.at[s, g], dr_sem.at[s, g], other)
            shares[s, g].start()
        if g == 1:
            loads[9].wait()
            loads[10].wait()
    for copy in shares.values():
        copy.wait_recv()

    block = lat // 4

    def latent_kv(q):
        acc_k = acc_v = None
        for part in range(parts):
            held = q if part % N_STREAMS == 0 else {0: 0, 1: 2, 2: 1, 3: 3}[q]
            x = lr[part, held * quarter:(held + 1) * quarter].reshape(block, span)
            k = mm(x, v_wlk[part * span:(part + 1) * span])
            v = mm(x, v_wlv[part * span:(part + 1) * span])
            acc_k = k if acc_k is None else acc_k + k
            acc_v = v if acc_v is None else acc_v + v
        flipped = acc_v.T.astype(BF16)
        for h in range(heads):
            cut = slice(h * HEAD_DIM, (h + 1) * HEAD_DIM)
            lkeys[h, q * block:(q + 1) * block] = acc_k[:, cut].astype(BF16)
            lvalt[h, :, q * block:(q + 1) * block] = flipped[cut]

    for q in range(4):
        latent_kv(q)

    def decode(i, _):
        h = i % heads
        start = pl.multiple_of((i // heads) * rows, rows)
        _, total, summed = attend(lkeys[h], pqt[h, :, pl.ds(start, rows)], lvalt[h], None)
        pa[h, pl.ds(start, rows)] = (summed / total).T.astype(BF16)
        return 0

    half = pos // 2
    loads[11].wait()

    def terms(start, size):
        joined = jnp.concatenate([pa[h, pl.ds(start, size)] for h in range(heads)], axis=1)
        return mm(joined, v_wpo[...])

    per_half = half // rows
    theirs = (1 - core) * per_half
    mine = core * per_half
    swaps = []
    for i in range(per_half):
        lax.fori_loop((theirs + i) * heads, (theirs + i + 1) * heads, decode, 0)
        start = pl.multiple_of((theirs + i) * rows, rows)
        tsend[i] = terms(start, rows).astype(BF16)
        copy = remote(tsend.at[i], trecv.at[i], x_sem.at[2 + 2 * i], x_sem.at[3 + 2 * i], other)
        copy.start()
        swaps.append(copy)
    for i in range(per_half):
        lax.fori_loop((mine + i) * heads, (mine + i + 1) * heads, decode, 0)
        start = pl.multiple_of((mine + i) * rows, rows)
        own_terms = terms(start, rows).astype(BF16).astype(F32)
        swaps[i].wait_recv()
        out[i * rows:(i + 1) * rows] = rms_norm(own_terms + trecv[i].astype(F32)).astype(BF16)
    for copy in swaps:
        copy.wait_send()
    for o, st in sent:
        o.wait_send()
        st.wait_send()
    gather_l.finish()
    for copy in shares.values():
        copy.wait_send()


def per_device(n, inputs, valid_blocks, latents, *weights):
    pos, width = inputs.shape
    lat_local = latents.shape[0]
    columns = weights[0].shape[1]
    heads = columns // HEAD_DIM
    hs = heads // N_STREAMS
    lat = n * lat_local
    bits = n.bit_length() - 1
    rows = min(pos, 256)
    per_half = pos // 2 // rows
    block = pos // valid_blocks.shape[0]
    bias = jnp.where(jnp.repeat(valid_blocks, block) > 0, 0.0, masked_score).astype(F32)
    bias = jnp.broadcast_to(bias[:, None], (pos, lat_local))
    operands = (inputs, bias, latents) + weights
    landed = [pltpu.VMEM(a.shape, a.dtype) for a in operands]
    dma = pltpu.SemaphoreType.DMA
    n_recv = n
    scratch = landed + [
        pltpu.VMEM((N_STREAMS, n, hs, HEAD_DIM, lat_local), BF16),
        pltpu.VMEM((heads, pos, HEAD_DIM), BF16),
        pltpu.VMEM((heads, HEAD_DIM, pos), BF16),
        pltpu.VMEM((heads, HEAD_DIM, pos), BF16),
        pltpu.VMEM((N_STREAMS, n, hs, HEAD_DIM, lat_local), BF16),
        pltpu.VMEM((N_STREAMS, n, hs, 2, lat_local), F32),
        pltpu.VMEM((N_STREAMS, n_recv, hs, HEAD_DIM, lat_local), BF16),
        pltpu.VMEM((N_STREAMS, n_recv, hs, 2, lat_local), F32),
        pltpu.VMEM((2 * N_STREAMS, n, lat_local, width // (2 * N_STREAMS)), BF16),
        pltpu.VMEM((heads, lat, HEAD_DIM), BF16),
        pltpu.VMEM((heads, HEAD_DIM, lat), BF16),
        pltpu.VMEM((heads, pos, HEAD_DIM), BF16),
        pltpu.VMEM((per_half, rows, width), BF16),
        pltpu.VMEM((per_half, rows, width), BF16),
        pltpu.VMEM((lat_local, width), BF16),
        pltpu.VMEM((lat_local, width), BF16),
        dma((len(operands),)),
        dma((N_STREAMS, bits, bits)),
        dma((N_STREAMS, bits, bits)),
        dma((N_STREAMS, bits, bits)),
        dma((N_STREAMS, bits, bits)),
        dma((N_STREAMS, bits + 1)),
        dma((N_STREAMS, bits + 1)),
        dma((N_STREAMS, bits, 2)),
        dma((N_STREAMS, bits, 2)),
        dma((N_STREAMS, bits, 2)),
        dma((N_STREAMS, bits, 2)),
        dma((2 + 2 * per_half,)),
    ]
    return pl.pallas_call(
        functools.partial(kernel, n),
        out_shape=jax.ShapeDtypeStruct((pos // 2, width), BF16),
        in_specs=[pl.BlockSpec(memory_space=pl.ANY)] * len(operands),
        out_specs=pl.BlockSpec(memory_space=pltpu.VMEM),
        scratch_shapes=scratch,
        compiler_params=pltpu.CompilerParams(
            collective_id=0, has_side_effects=True, vmem_limit_bytes=60 * 1024 * 1024),
        name="perceiver",
    )(*operands)


def solution(mesh):
    placed = (
        P("pos", None),
        P("pos"),
        P("pos", None),
        P(None, "head"),
        P(None, "head"),
        P(None, "head"),
        P("head", None),
        P(),
        P(None, "head"),
        P(None, "head"),
        P(None, "head"),
        P("head", None),
    )
    return jax.shard_map(
        functools.partial(per_device, mesh.shape["pos"]), mesh=mesh, in_specs=placed,
        out_specs=P(("pos", "head"), None), check_vma=False
    )
```

time: 574 us -> 120 us (0.21)
  waiting for transfers between devices: 317 us -> 0 us
  Pallas kernels: 0 us -> 116 us
  blocking collectives: 115 us -> 0 us
  matrix products: 72.4 us -> 0 us
  other arithmetic: 34.7 us -> 0.66 us
  local copies, waits for them, and re-layouts: 19.2 us -> 3.33 us
  between operations: 13.7 us -> 0.01 us
    all_gather x3 -> x0, waiting for transfers between devices: 164 us -> none  [the longest x1 58.7 us: per_device(): lax.all_gather(lat_keys, 'pos', axis=0, tiled=True)]
    psum x2 -> x0, waiting for transfers between devices: 143 us -> none  [the longest x1 124 us: per_device(): all_totals, all_sums = lax.psum((scaled_totals, scaled_sums), 'pos')]
    pallas_call x0 -> x1, Pallas kernels: none -> 116 us  [per_device(): pl.pallas_call(functools.partial(kernel, n), out_shape=jax.ShapeDtypeStru...]
    dot_general x17 -> x0, matrix products: 72.4 us -> none  [the longest x2 24 us: cross_block(): jnp.einsum('lhp,phe->lhe', exponent.astype(jnp.bfloat16), pos_values, pre...]
    psum x1 -> x0, blocking collectives: 60.9 us -> none  [per_device(): all_totals, all_sums = lax.psum((scaled_totals, scaled_sums), 'pos')]
    pmax x1 -> x0, blocking collectives: 54.2 us -> none  [per_device(): lax.pmax(row_max.astype(jnp.bfloat16), 'pos').astype(row_max.dtype)]
    reduce_sum x6 -> x0, other arithmetic: 24.9 us -> none  [the longest x2 15.8 us: cross_block(): totals = jnp.sum(exponent, axis=-1)]
    reduce_scatter x1 -> x0, waiting for transfers between devices: 9.72 us -> none  [per_device(): lax.psum_scatter(terms.astype(jnp.bfloat16), 'head', scatter_dimension=0,...]
  transfers between devices with their start and end apart: 6 -> 0, of which waited for: 6 -> 0; matrix products, arithmetic and copies ran while one was open for 4% -> 0% of each run, Pallas kernels for 0% -> 0%
where the time goes in v1:
time: 120 us
  Pallas kernels  116 us (97%)
  local copies, waits for them, and re-layouts  3.33 us (3%)
    pallas_call x1, Pallas kernels, per_device(): pl.pallas_call(functools.partial(kernel, n), out_shape=jax.ShapeDtypeStru...  116 us

profile of v1, /device:TPU:9, one launch (start us, length us, event | category | flops | bytes accessed | tf_op | source)
XLA Modules:
  0.0 119.8 jit_solution(15710383363443452710)
XLA Ops:
  0.0 0.7 compare_select_fusion
  0.7 0.1 broadcast_bitcast_fusion
  0.7 1.0 broadcast_in_dim.20.bias
  1.7 115.8 %perceiver.1 = bf16[512,1024]{1,0:T(8,128)(2,1)} custom-call(bf16[1024,1024]{1,0:T(8,128)(2,1)} %inputs.1, f32[1024,128]{1,0:T(8,128)} %broadcast_in_dim.20.bias, bf16[128,1024]{1,0:T(8,128)(2,1)} %latents.1, bf16[1024,512]{1,0:T(8,128)(2,1)} %w_query.1, bf16[1024,512]{1,0:T(8,128)(2,1)} %w_key.1, bf16[1024,512]{1,0:T(8,128)(2,1)} %w_value.1, ...), custom_call_target="tpu_custom_call" | custom-call | tf_op jit(solution)/shard_map/perceiver/pallas_call | solution.py:385
  117.6 2.3 %copy.14 = bf16[512,1024]{1,0:T(8,128)(2,1)} copy(bf16[512,1024]{1,0:T(8,128)(2,1)} %perceiver.1) | data formatting | bytes 2097152

commit v2 on v1

--- a/solution.py
+++ b/solution.py
@@ -32,7 +32,7 @@
 def kernel(n, inputs, bias, latents, w_query, w_key, w_value, w_out, w_mlp, w_lkey, w_lvalue,
            w_pquery, w_pout, out,
            v_in, v_bias, v_lat, v_wq, v_wk, v_wv, v_wo, v_wm, v_wlk, v_wlv, v_wpq, v_wpo,
-           qt, keys, valt, pqt, osum, stats, orecv, srecv, lr, lkeys, lvalt, pa,
+           qt, keys, valt, pqt, osum, stats, orecv, srecv, lr, lkeys, lvalt, pa, dstat, dsum,
            tsend, trecv, msend, mrecv,
            load_sem, gs_sem, gr_sem, hs_sem, hr_sem, ds_sem, dr_sem,
            os_sem, or_sem, ss_sem, sr_sem, x_sem):
@@ -193,21 +193,20 @@
             o.wait_recv()
             st.wait_recv()
 
-        def body(i, _):
-            h = i % heads
-            r = i // heads
-            s, hh = h // hs, h % hs
-            mine, theirs = stats[s, a + r, hh], srecv[s, base + r, hh]
-            top = jnp.maximum(mine[0:1], theirs[0:1])
-            f, g = jnp.exp2(mine[0:1] - top), jnp.exp2(theirs[0:1] - top)
-            stats[s, a + r, hh, 0:1] = top
-            stats[s, a + r, hh, 1:2] = mine[1:2] * f + theirs[1:2] * g
-            osum[s, a + r, hh] = (
-                osum[s, a + r, hh].astype(F32) * f + orecv[s, base + r, hh].astype(F32) * g
-            ).astype(BF16)
+        def body(r, _):
+            for h in range(heads):
+                s, hh = h // hs, h % hs
+                mine, theirs = stats[s, a + r, hh], srecv[s, base + r, hh]
+                top = jnp.maximum(mine[0:1], theirs[0:1])
+                f, g = jnp.exp2(mine[0:1] - top), jnp.exp2(theirs[0:1] - top)
+                stats[s, a + r, hh, 0:1] = top
+                stats[s, a + r, hh, 1:2] = mine[1:2] * f + theirs[1:2] * g
+                osum[s, a + r, hh] = (
+                    osum[s, a + r, hh].astype(F32) * f + orecv[s, base + r, hh].astype(F32) * g
+                ).astype(BF16)
             return 0
 
-        lax.fori_loop(0, heads * (b - a), body, 0)
+        lax.fori_loop(0, b - a, body, 0)
 
     loads[5].wait()
     encode(0)
@@ -253,53 +252,79 @@
     normed = rms_norm(msend[...].astype(F32) + mrecv[...].astype(F32))
     hidden = jax.nn.gelu(mm(normed.astype(BF16), v_wm[...]))
     lat_rows = (normed + hidden).astype(BF16)
-    parts = lr.shape[0]
-    span = width // parts
-    for q in range(parts):
-        lr[q, 0] = lat_rows[:, q * span:(q + 1) * span]
-
-    gather_l = Gather(lambda s, a, b: lr.at[core * N_STREAMS + s, a:b], hs_sem, hr_sem)
-    gather_l.ready(0)
+    part_rows = lat_local // N_STREAMS
+    span = width // 2
+    for s in range(N_STREAMS):
+        for c in range(2):
+            lr[c, s, 0] = lat_rows[s * part_rows:(s + 1) * part_rows, c * span:(c + 1) * span]
+
+    gather_l = Gather(lambda s, a, b: lr.at[core, s, a:b], hs_sem, hr_sem)
     shares = {}
-    for g in range(1, bits + 1):
+    block = quarter * part_rows
+
+    def share(g):
         gather_l.ready(g)
         a, b = group(g)
         for s in range(N_STREAMS):
-            view = lr.at[core * N_STREAMS + s, a:b]
+            view = lr.at[core, s, a:b]
             shares[s, g] = remote(view, view, ds_sem.at[s, g], dr_sem.at[s, g], other)
             shares[s, g].start()
-        if g == 1:
-            loads[9].wait()
-            loads[10].wait()
-    for copy in shares.values():
-        copy.wait_recv()
-
-    block = lat // 4
+
+    def shared(g):
+        for s in range(N_STREAMS):
+            shares[s, g].wait_recv()
 
     def latent_kv(q):
-        acc_k = acc_v = None
-        for part in range(parts):
-            held = q if part % N_STREAMS == 0 else {0: 0, 1: 2, 2: 1, 3: 3}[q]
-            x = lr[part, held * quarter:(held + 1) * quarter].reshape(block, span)
-            k = mm(x, v_wlk[part * span:(part + 1) * span])
-            v = mm(x, v_wlv[part * span:(part + 1) * span])
-            acc_k = k if acc_k is None else acc_k + k
-            acc_v = v if acc_v is None else acc_v + v
-        flipped = acc_v.T.astype(BF16)
-        for h in range(heads):
-            cut = slice(h * HEAD_DIM, (h + 1) * HEAD_DIM)
-            lkeys[h, q * block:(q + 1) * block] = acc_k[:, cut].astype(BF16)
-            lvalt[h, :, q * block:(q + 1) * block] = flipped[cut]
-
-    for q in range(4):
-        latent_kv(q)
+        for s in range(N_STREAMS):
+            at = (q * N_STREAMS + s) * block
+            x = jnp.concatenate(
+                [lr[c, s, q * quarter:(q + 1) * quarter].reshape(block, span) for c in range(2)],
+                axis=1)
+            k = mm(x, v_wlk[...]).astype(BF16)
+            flipped = mm(x, v_wlv[...]).T.astype(BF16)
+            for h in range(heads):
+                cut = slice(h * HEAD_DIM, (h + 1) * HEAD_DIM)
+                lkeys[h, at:at + block] = k[:, cut]
+                lvalt[h, :, at:at + block] = flipped[cut]
+
+    def decode_first(i, _):
+        h = i % heads
+        start = pl.multiple_of((i // heads) * rows, rows)
+        top, total, summed = attend(
+            lkeys[h, :lat // 2], pqt[h, :, pl.ds(start, rows)], lvalt[h, :, :lat // 2], None)
+        dstat[h, i // heads, 0:1] = top
+        dstat[h, i // heads, 1:2] = total
+        dsum[h, i // heads] = summed
+        return 0
 
     def decode(i, _):
         h = i % heads
         start = pl.multiple_of((i // heads) * rows, rows)
-        _, total, summed = attend(lkeys[h], pqt[h, :, pl.ds(start, rows)], lvalt[h], None)
-        pa[h, pl.ds(start, rows)] = (summed / total).T.astype(BF16)
+        top, total, summed = attend(
+            lkeys[h, lat // 2:], pqt[h, :, pl.ds(start, rows)], lvalt[h, :, lat // 2:], None)
+        before = dstat[h, i // heads]
+        peak = jnp.maximum(top, before[0:1])
+        f, g = jnp.exp2(before[0:1] - peak), jnp.exp2(top - peak)
+        scaled = dsum[h, i // heads] * f + summed * g
+        pa[h, pl.ds(start, rows)] = (scaled / (before[1:2] * f + total * g)).T.astype(BF16)
         return 0
+
+    gather_l.ready(0)
+    for g in range(1, bits - 1):
+        share(g)
+    loads[9].wait()
+    loads[10].wait()
+    for g in range(1, bits - 1):
+        shared(g)
+    latent_kv(0)
+    share(bits - 1)
+    shared(bits - 1)
+    latent_kv(1)
+    lax.fori_loop(0, pos // rows * heads, decode_first, 0)
+    share(bits)
+    shared(bits)
+    latent_kv(2)
+    latent_kv(3)
 
     half = pos // 2
     loads[11].wait()
@@ -361,10 +386,12 @@
         pltpu.VMEM((N_STREAMS, n, hs, 2, lat_local), F32),
         pltpu.VMEM((N_STREAMS, n_recv, hs, HEAD_DIM, lat_local), BF16),
         pltpu.VMEM((N_STREAMS, n_recv, hs, 2, lat_local), F32),
-        pltpu.VMEM((2 * N_STREAMS, n, lat_local, width // (2 * N_STREAMS)), BF16),
+        pltpu.VMEM((2, N_STREAMS, n, lat_local // N_STREAMS, width // 2), BF16),
         pltpu.VMEM((heads, lat, HEAD_DIM), BF16),
         pltpu.VMEM((heads, HEAD_DIM, lat), BF16),
         pltpu.VMEM((heads, pos, HEAD_DIM), BF16),
+        pltpu.VMEM((heads, pos // rows, 2, rows), F32),
+        pltpu.VMEM((heads, pos // rows, HEAD_DIM, rows), F32),
         pltpu.VMEM((per_half, rows, width), BF16),
         pltpu.VMEM((per_half, rows, width), BF16),
         pltpu.VMEM((lat_local, width), BF16),

time: 120 us -> 118 us (0.983); the launches traced: 120 us -> 116 us
  Pallas kernels: 116 us -> 112 us
    pallas_call x1, Pallas kernels: 116 us -> 112 us  [per_device(): pl.pallas_call(functools.partial(kernel, n), out_shape=jax.ShapeDtypeStru...]
where the time goes in v2:
time: 118 us; the launch traced here: 116 us
  Pallas kernels  112 us (95%)
  local copies, waits for them, and re-layouts  3.33 us (3%)
    pallas_call x1, Pallas kernels, per_device(): pl.pallas_call(functools.partial(kernel, n), out_shape=jax.ShapeDtypeStru...  112 us

profile of v2, /device:TPU:9, one launch (start us, length us, event | category | flops | bytes accessed | tf_op | source)
XLA Modules:
  0.0 116.4 jit_solution(1724329305320883108)
XLA Ops:
  0.0 0.7 compare_select_fusion
  0.7 0.1 broadcast_bitcast_fusion
  0.7 1.0 broadcast_in_dim.20.bias
  1.7 112.4 %perceiver.1 = bf16[512,1024]{1,0:T(8,128)(2,1)} custom-call(bf16[1024,1024]{1,0:T(8,128)(2,1)} %inputs.1, f32[1024,128]{1,0:T(8,128)} %broadcast_in_dim.20.bias, bf16[128,1024]{1,0:T(8,128)(2,1)} %latents.1, bf16[1024,512]{1,0:T(8,128)(2,1)} %w_query.1, bf16[1024,512]{1,0:T(8,128)(2,1)} %w_key.1, bf16[1024,512]{1,0:T(8,128)(2,1)} %w_value.1, ...), custom_call_target="tpu_custom_call" | custom-call | tf_op jit(solution)/shard_map/perceiver/pallas_call | solution.py:412
  114.1 2.3 %copy.14 = bf16[512,1024]{1,0:T(8,128)(2,1)} copy(bf16[512,1024]{1,0:T(8,128)(2,1)} %perceiver.1) | data formatting | bytes 2097152
